TPU v7x, 32 devices: a whole 2x2x4 slice. The times are simulated.
32 devices in a mesh: groups: 2 (over y), img: 4 (over z), filt: 2 (over x), chan: 2 (over core).
Axes of the slice: x: 2, y: 2, z: 4, core: 2. Of those that a mesh axis runs over, the one named last changes fastest.
Arguments:
- images: float32 [16, 3, 32, 128], P(('groups', 'img', 'chan')), parts along dimension 0, may hold values from -24 to 24
- coefficients: bfloat16 [16, 256, 32, 128], P(('groups', 'img', 'chan'), 'filt'), parts along dimension 0, may hold values from -1.5 to 1.5
- dictionary: float32 [256, 363], P(('filt', 'img')), may hold values from -0.3 to 0.3
Outputs:
- coefficients_out: bfloat16 [16, 256, 32, 128], P(('groups', 'img', 'chan'), 'filt'), parts along dimension 0
- dictionary_out: float32 [512, 363], P(('groups', 'filt', 'img')), parts along dimension 0
There are 2 independent parts, one for each index of `groups`. A program takes and returns all parts, laid end to end along the dimension named above; an argument that names none is the same for every part. Nothing has to cross between parts.
All inputs are finite; a program needn't handle non-finite values.
Results may differ from a plain program's by a relative error of at most 0.018.
Values may be sent and summed in bfloat16 or wider, within the bound.
A program may use at most 128 MiB of HBM per device.

v0:
```python
import functools
import jax
import jax.numpy as jnp
import numpy as np
from jax import lax
from jax.experimental import pallas as pl
from jax.experimental.pallas import tpu as pltpu
from jax.sharding import PartitionSpec as P

ITERS = 2
SIDE = 11
HALF = SIDE // 2
COLORS = 3
CODE_STEP = 0.04
SHRINK = 0.15
FILTER_STEP = 0.02
EPSILON = 1e-06

BLOCK = 40
ROWS = 448
GROUP = 8
SPAN = GROUP + SIDE - 1
LANES = 128
MESH = pl.DeviceIdType.MESH
F32 = jnp.float32
BF16 = jnp.bfloat16


def tap_order(taps, width):
    order = np.zeros((width, ROWS), np.float32)
    for tap in range(taps):
        color, rest = divmod(tap, SIDE * SIDE)
        row, col = divmod(rest, SIDE)
        order[tap, col * BLOCK + row * COLORS + color] = 1.0
    return order.astype(jnp.bfloat16)


def roll_columns(values, shift):
    if shift == 0:
        return values
    column = lax.broadcasted_iota(jnp.int32, values.shape, 1)
    rolled = pltpu.roll(values, shift % LANES, 1)
    inside = (column >= shift) & (column < LANES + shift)
    return jnp.where(inside, rolled, 0.0)


def kernel(
    sizes, count,
    img_ref, coef_hbm, dict_ref, order_ref,
    cout_ref, dout_ref,
    cpad, patches, toep, dtp, xb, image_rows,
    fil_bf, fil32, rec, gtx, grx, gall, glast, sqs,
    local_sem, send_sem, recv_sem,
):
    n_img, n_filt, n_chan = sizes
    n = n_img * n_chan
    n_part = n * n_filt
    height, width = img_ref.shape[1], img_ref.shape[2]
    pixels = height * width
    rows = height * COLORS
    kp = cpad.shape[0]
    share = fil32.shape[1]
    piece = share // n_chan
    taps = dict_ref.shape[1]
    groups = height // GROUP
    gr = GROUP * COLORS

    img, filt, chan = (lax.axis_index(a) for a in ("img", "filt", "chan"))
    me = img * n_chan + chan
    me_part = me * n_filt + filt

    def img_peers():
        return [{"img": lax.rem(img + s, n_img)} for s in range(1, n_img)]

    def filt_peers():
        return [{"filt": lax.rem(filt + s, n_filt)} for s in range(1, n_filt)]

    def chan_peers():
        return [{"chan": lax.rem(chan + s, n_chan)} for s in range(1, n_chan)]

    def set_peers():
        peers = []
        for s in range(1, n):
            other = lax.rem(me + s, n)
            peers.append((other, {"img": other // n_chan, "chan": lax.rem(other, n_chan)}))
        return peers

    def part_loop(body):
        def step(s, carry):
            other = lax.rem(me_part + s, n_part)
            place = other // n_filt
            body({
                "img": place // n_chan,
                "chan": lax.rem(place, n_chan),
                "filt": lax.rem(other, n_filt),
            })
            return carry
        lax.fori_loop(1, n_part, step, 0)

    def push(src, dst, sem, device):
        pltpu.make_async_remote_copy(
            src_ref=src, dst_ref=dst, send_sem=send_sem.at[sem], recv_sem=recv_sem.at[sem],
            device_id=device, device_id_type=MESH,
        ).start()

    def wait_in(view, sem):
        pltpu.make_async_copy(view, view, recv_sem.at[sem]).wait()

    def wait_out(view, sem):
        pltpu.make_async_copy(view, view, send_sem.at[sem]).wait()

    load = pltpu.make_async_copy(
        coef_hbm, cpad.at[:, pl.ds(HALF * width, pixels)], local_sem
    )
    load.start()

    barrier = pltpu.get_barrier_semaphore()
    part_loop(lambda d: pl.semaphore_signal(barrier, inc=1, device_id=d, device_id_type=MESH))

    own = jnp.zeros((share, fil32.shape[2]), F32)
    fil32[img] = own
    fil32[img, :, :taps] = dict_ref[...]
    fil_bf[img] = fil32[img].astype(BF16)

    edge = HALF * width
    cpad[:, :edge] = jnp.zeros((kp, edge), BF16)
    cpad[:, edge + pixels:] = jnp.zeros((kp, cpad.shape[1] - edge - pixels), BF16)
    dtp[...] = jnp.zeros(dtp.shape, F32)
    xb[...] = jnp.zeros(xb.shape, F32)
    for color in range(COLORS):
        image_rows[pl.ds(color, height, stride=COLORS), :] = img_ref[color]

    pl.semaphore_wait(barrier, n_part - 1)
    for d in img_peers():
        push(fil_bf.at[img], fil_bf.at[img], 0, d)
    for d in img_peers():
        push(fil32.at[img], fil32.at[img], 1, d)
    if n_img > 1:
        wait_in(fil_bf.at[pl.ds(0, n_img - 1)], 0)

    filters = fil_bf[...].reshape(kp, fil_bf.shape[2])
    for it in range(ITERS):
        last = it == ITERS - 1
        base = 2 + it * 4
        ordered = jnp.dot(filters, order_ref[...], preferred_element_type=F32)
        flipped = ordered.T
        for col in range(SIDE):
            dtp[col, gr:gr + BLOCK, :] = flipped[col * BLOCK:(col + 1) * BLOCK]
        for row in range(SPAN):
            start = gr + COLORS * (SIDE - 1 - row)
            parts = [dtp[col, start:start + gr, :] for col in range(SIDE)]
            spare = toep.shape[0] - SIDE * gr
            parts.append(jnp.zeros((spare, kp), F32))
            toep[:, row * kp:(row + 1) * kp] = jnp.concatenate(parts, 0).astype(BF16)
        if it == 0:
            load.wait()
        shifted = jnp.concatenate([
            jnp.concatenate([
                cpad[:, (g * GROUP + row) * width:(g * GROUP + row + 1) * width]
                for g in range(groups)
            ], 1) for row in range(SPAN)
        ], 0)
        summed = jnp.dot(toep[...], shifted, preferred_element_type=F32)
        share_sum = None
        for col in range(SIDE):
            block = jnp.concatenate([
                summed[col * gr:(col + 1) * gr, g * width:(g + 1) * width] for g in range(groups)
            ], 0)
            term = roll_columns(block, col - HALF)
            share_sum = term if share_sum is None else share_sum + term
        rec[it, filt] = share_sum
        for d in filt_peers():
            push(rec.at[it, filt], rec.at[it, filt], base, d)
        if n_filt > 1:
            wait_in(rec.at[it, pl.ds(0, n_filt - 1)], base)
        recon = rec[it, 0]
        for f in range(1, n_filt):
            recon = recon + rec[it, f]
        resid = (recon - image_rows[...]).astype(BF16).astype(F32)

        for col in range(SIDE):
            xb[col, 16:16 + rows, :] = roll_columns(resid, HALF - col)
        for y in range(height):
            start = COLORS * y + 1
            parts = [xb[col, start:start + BLOCK, :] for col in range(SIDE)]
            parts.append(jnp.zeros((ROWS - SIDE * BLOCK, width), F32))
            patches[:, y * width:(y + 1) * width] = jnp.concatenate(parts, 0).astype(BF16)

        grad = lax.dot_general(
            cpad[:, edge:edge + pixels], patches[...], (((1,), (1,)), ((), ())),
            preferred_element_type=F32,
        )
        plain = lax.dot_general(
            grad.astype(BF16), order_ref[...], (((1,), (1,)), ((), ())),
            preferred_element_type=F32,
        ).astype(BF16)
        gtx[it] = plain.reshape(n, piece, plain.shape[1])
        grx[it, me] = gtx[it, me]
        for other, d in set_peers():
            push(gtx.at[it, other], grx.at[it, me], base + 1, d)

        ordered_bf = ordered.astype(BF16)
        step = 4 * width
        for start in range(0, pixels, step):
            moved = cpad[:, edge + start:edge + start + step].astype(F32) - CODE_STEP * jnp.dot(
                ordered_bf, patches[:, start:start + step], preferred_element_type=F32
            )
            fresh = (moved - jnp.clip(moved, -SHRINK, SHRINK)).astype(BF16)
            if last:
                cout_ref[:, start:start + step] = fresh
            else:
                cpad[:, edge + start:edge + start + step] = fresh

        if n > 1:
            wait_in(grx.at[it, pl.ds(0, n - 1)], base + 1)
        total = grx[it, 0].astype(F32)
        for s in range(1, n):
            total = total + grx[it, s].astype(F32)
        total_bf = total.astype(BF16)
        total = total_bf.astype(F32)
        square = jnp.sum(jnp.sum(total * total, axis=1, keepdims=True), axis=0, keepdims=True)
        sqs[it, me_part] = jnp.broadcast_to(square, sqs.shape[2:])
        part_loop(lambda d: push(sqs.at[it, me_part], sqs.at[it, me_part], base + 3, d))
        if last:
            glast[chan] = total_bf
            for d in chan_peers():
                push(glast.at[chan], glast.at[chan], base + 2, d)
            if n_chan > 1:
                wait_in(glast.at[pl.ds(0, n_chan - 1)], base + 2)
            gradient = glast[...].reshape(share, glast.shape[2]).astype(F32)
            current = fil32[img]
        else:
            gall[it, me] = total_bf
            for other, d in set_peers():
                push(gall.at[it, me], gall.at[it, me], base + 2, d)
            if it == 0 and n_img > 1:
                wait_in(fil32.at[pl.ds(0, n_img - 1)], 1)
                wait_out(fil32.at[pl.ds(0, n_img - 1)], 1)
            if n > 1:
                wait_in(gall.at[it, pl.ds(0, n - 1)], base + 2)
            gradient = gall[it].reshape(kp, gall.shape[3]).astype(F32)
            current = fil32[...].reshape(kp, fil32.shape[2])
        if n_part > 1:
            wait_in(sqs.at[it, pl.ds(0, n_part - 1)], base + 3)
        squares = jnp.sum(sqs[it], axis=0)[:1, :1]
        scale = jnp.sqrt(squares / count + EPSILON)
        moved = current - FILTER_STEP * gradient / scale
        lengths = jnp.sqrt(jnp.sum(moved * moved, axis=1, keepdims=True))
        moved = moved / jnp.maximum(lengths, 1.0)
        if last:
            dout_ref[...] = moved[:, :taps]
        else:
            fil32[...] = moved.reshape(fil32.shape)
            filters = moved.astype(BF16)

    if n_img > 1:
        wait_out(fil_bf.at[pl.ds(0, n_img - 1)], 0)
    for it in range(ITERS):
        base = 2 + it * 4
        if n_filt > 1:
            wait_out(rec.at[it, pl.ds(0, n_filt - 1)], base)
        if n > 1:
            wait_out(grx.at[it, pl.ds(0, n - 1)], base + 1)
        if it == ITERS - 1:
            if n_chan > 1:
                wait_out(glast.at[pl.ds(0, n_chan - 1)], base + 2)
        elif n > 1:
            wait_out(gall.at[it, pl.ds(0, n - 1)], base + 2)
        if n_part > 1:
            wait_out(sqs.at[it, pl.ds(0, n_part - 1)], base + 3)


def per_device(sizes, images, coefficients, dictionary):
    n_img, n_filt, n_chan = sizes
    n = n_img * n_chan
    _, filters, height, width = coefficients.shape
    held, taps = dictionary.shape
    pixels = height * width
    share = -(-held // (16 * n_chan)) * 16 * n_chan
    kp = share * n_img
    lanes = -(-taps // LANES) * LANES
    coef = coefficients.reshape(n_img, held, pixels)
    coef = jnp.pad(coef, ((0, 0), (0, share - held), (0, 0))).reshape(kp, pixels)
    dictionary = jnp.pad(dictionary, ((0, share - held), (0, 0)))
    order = jnp.asarray(tap_order(taps, lanes))
    gr = GROUP * COLORS
    toep_rows = -(-SIDE * gr // 16) * 16
    dtp_rows = gr + COLORS * (SIDE - 1) + gr + 2
    sems = 2 + 4 * ITERS
    vmem = pl.BlockSpec(memory_space=pltpu.VMEM)
    out_coef, out_dict = pl.pallas_call(
        functools.partial(kernel, sizes, float(filters * n_filt * taps)),
        out_shape=(
            jax.ShapeDtypeStruct((kp, pixels), BF16),
            jax.ShapeDtypeStruct((share, taps), F32),
        ),
        in_specs=[vmem, pl.BlockSpec(memory_space=pl.ANY), vmem, vmem],
        out_specs=(vmem, vmem),
        scratch_shapes=[
            pltpu.VMEM((kp, (height + 2 * HALF) * width), BF16),
            pltpu.VMEM((ROWS, pixels), BF16),
            pltpu.VMEM((toep_rows, SPAN * kp), BF16),
            pltpu.VMEM((SIDE, dtp_rows, kp), F32),
            pltpu.VMEM((SIDE, COLORS * (height - 1) + BLOCK + 3, width), F32),
            pltpu.VMEM((COLORS * height, width), F32),
            pltpu.VMEM((n_img, share, lanes), BF16),
            pltpu.VMEM((n_img, share, lanes), F32),
            pltpu.VMEM((ITERS, n_filt, COLORS * height, width), F32),
            pltpu.VMEM((ITERS, n, share // n_chan, lanes), BF16),
            pltpu.VMEM((ITERS, n, share // n_chan, lanes), BF16),
            pltpu.VMEM((ITERS - 1, n, share // n_chan, lanes), BF16),
            pltpu.VMEM((n_chan, share // n_chan, lanes), BF16),
            pltpu.VMEM((ITERS, n * n_filt, 8, LANES), F32),
            pltpu.SemaphoreType.DMA,
            pltpu.SemaphoreType.DMA((sems,)),
            pltpu.SemaphoreType.DMA((sems,)),
        ],
        compiler_params=pltpu.CompilerParams(
            collective_id=0, has_side_effects=True, vmem_limit_bytes=56 * 2**20
        ),
        name="dictionary_steps",
    )(images[0], coef, dictionary, order)
    out_coef = out_coef.reshape(n_img, share, height, width)[:, :held]
    return out_coef.reshape(1, filters, height, width), out_dict[:held]


def solution(mesh):
    sizes = tuple(mesh.shape[a] for a in ("img", "filt", "chan"))
    placed = (
        P(("groups", "img", "chan"), None, None, None),
        P(("groups", "img", "chan"), "filt", None, None),
        P(("filt", "img"), None),
    )
    return jax.shard_map(
        functools.partial(per_device, sizes),
        mesh=mesh,
        in_specs=placed,
        out_specs=(
            P(("groups", "img", "chan"), "filt", None, None),
            P(("groups", "filt", "img"), None),
        ),
        check_vma=False,
    )
```

profile of v0, /device:TPU:0, one launch (start us, length us, event | category | flops | bytes accessed | tf_op | source)
XLA Modules:
  0.0 49.5 jit_solution(12639273214718022223)
XLA Ops:
  0.6 2.6 %copy.9 = bf16[16,8,32,128]{3,1,2,0:T(8,128)(2,1)} copy(bf16[16,8,32,128]{3,2,1,0:T(8,128)(2,1)} %bitcast.10) | data formatting | bytes 2097152
  3.3 43.2 %dictionary_steps.1 = (bf16[128,4096]{1,0:T(8,128)(2,1)}, f32[32,363]{1,0:T(8,128)}) custom-call(f32[3,32,128]{2,1,0:T(8,128)} %bitcast.13, bf16[128,4096]{1,0:T(8,128)(2,1)} %bitcast.9, f32[32,363]{1,0:T(8,128)} %dict_ref.1, bf16[384,448]{1,0:T(8,128)(2,1)} %constant.1.clone.order_ref), custom_call_target="tpu_custom_call" | custom-call | tf_op jit(solution)/shard_map/dictionary_steps/pallas_call | solution.py:291
  46.5 0.0 copy-start
  46.5 2.4 %copy.7 = bf16[16,8,32,128]{3,2,1,0:T(8,128)(2,1)} copy(bf16[16,8,32,128]{3,1,2,0:T(8,128)(2,1)} %bitcast.12) | data formatting | bytes 2097152
  48.9 0.0 copy-done
  48.9 0.6 %copy.11 = f32[32,363]{1,0:T(8,128)} copy(f32[32,363]{1,0:T(8,128)S(1)} %copy-done) | data formatting | bytes 92928
Async XLA Ops:
  46.5 2.5 %copy-start = (f32[32,363]{1,0:T(8,128)S(1)}, f32[32,363]{1,0:T(8,128)}, u32[]{:S(2)}) copy-start(f32[32,363]{1,0:T(8,128)} %get-tuple-element.9) | copy-start | bytes 139396
where the time goes:
time: 49.7 us; the launch traced here: 49.5 us
  Pallas kernels  43.2 us (87%)
  local copies, waits for them, and re-layouts  5.71 us (11%)
  between operations  0.65 us (1%)
    pallas_call x1, Pallas kernels, per_device(): pl.pallas_call(functools.partial(kernel, sizes, float(filters * n_filt *...  43.2 us
    unnamed x5, local copies, waits for them, and re-layouts  5.71 us

commit v1 on v0

--- a/solution.py
+++ b/solution.py
@@ -46,9 +46,9 @@
 
 def kernel(
     sizes, count,
-    img_ref, coef_hbm, dict_ref, order_ref,
-    cout_ref, dout_ref,
-    cpad, patches, toep, dtp, xb, image_rows,
+    img_ref, coef_hbm, dict_ref, order_hbm,
+    cout_hbm, dout_ref,
+    native, cpad, patches, toep, dtp, xb, image_rows, order_ref, fresh_rows, cout_bf,
     fil_bf, fil32, rec, gtx, grx, gall, glast, sqs,
     local_sem, send_sem, recv_sem,
 ):
@@ -87,7 +87,8 @@
 
     def part_loop(body):
         def step(s, carry):
-            other = lax.rem(me_part + s, n_part)
+            other = me_part + s
+            other = jnp.where(other >= n_part, other - n_part, other)
             place = other // n_filt
             body({
                 "img": place // n_chan,
@@ -95,7 +96,11 @@
                 "filt": lax.rem(other, n_filt),
             })
             return carry
-        lax.fori_loop(1, n_part, step, 0)
+        if n_part > 32:
+            lax.fori_loop(1, n_part, step, 0)
+        else:
+            for s in range(1, n_part):
+                step(s, 0)
 
     def push(src, dst, sem, device):
         pltpu.make_async_remote_copy(
@@ -109,12 +114,11 @@
     def wait_out(view, sem):
         pltpu.make_async_copy(view, view, send_sem.at[sem]).wait()
 
-    load = pltpu.make_async_copy(
-        coef_hbm, cpad.at[:, pl.ds(HALF * width, pixels)], local_sem
-    )
+    barrier = pltpu.get_barrier_semaphore()
+    load = pltpu.make_async_copy(coef_hbm, native, local_sem.at[0])
     load.start()
-
-    barrier = pltpu.get_barrier_semaphore()
+    load_order = pltpu.make_async_copy(order_hbm, order_ref, local_sem.at[1])
+    load_order.start()
     part_loop(lambda d: pl.semaphore_signal(barrier, inc=1, device_id=d, device_id_type=MESH))
 
     own = jnp.zeros((share, fil32.shape[2]), F32)
@@ -133,8 +137,13 @@
     pl.semaphore_wait(barrier, n_part - 1)
     for d in img_peers():
         push(fil_bf.at[img], fil_bf.at[img], 0, d)
-    for d in img_peers():
-        push(fil32.at[img], fil32.at[img], 1, d)
+    load.wait()
+    for y in range(0, height, 16):
+        fresh_rows[...] = native[:, y:y + 16, :].astype(F32)
+        for r in range(16):
+            at = edge + (y + r) * width
+            cpad[:, at:at + width] = fresh_rows[:, r, :].astype(BF16)
+    load_order.wait()
     if n_img > 1:
         wait_in(fil_bf.at[pl.ds(0, n_img - 1)], 0)
 
@@ -152,8 +161,6 @@
             spare = toep.shape[0] - SIDE * gr
             parts.append(jnp.zeros((spare, kp), F32))
             toep[:, row * kp:(row + 1) * kp] = jnp.concatenate(parts, 0).astype(BF16)
-        if it == 0:
-            load.wait()
         shifted = jnp.concatenate([
             jnp.concatenate([
                 cpad[:, (g * GROUP + row) * width:(g * GROUP + row + 1) * width]
@@ -171,6 +178,9 @@
         rec[it, filt] = share_sum
         for d in filt_peers():
             push(rec.at[it, filt], rec.at[it, filt], base, d)
+        if it == 0:
+            for d in img_peers():
+                push(fil32.at[img], fil32.at[img], 1, d)
         if n_filt > 1:
             wait_in(rec.at[it, pl.ds(0, n_filt - 1)], base)
         recon = rec[it, 0]
@@ -207,10 +217,17 @@
             )
             fresh = (moved - jnp.clip(moved, -SHRINK, SHRINK)).astype(BF16)
             if last:
-                cout_ref[:, start:start + step] = fresh
+                y = start // width
+                for r in range(4):
+                    fresh_rows[:, y % 16 + r, :] = fresh[:, r * width:(r + 1) * width].astype(F32)
+                if (y + 4) % 16 == 0:
+                    cout_bf[:, y - 12:y + 4, :] = fresh_rows[...].astype(BF16)
             else:
                 cpad[:, edge + start:edge + start + step] = fresh
 
+        if last:
+            store = pltpu.make_async_copy(cout_bf, cout_hbm, local_sem.at[0])
+            store.start()
         if n > 1:
             wait_in(grx.at[it, pl.ds(0, n - 1)], base + 1)
         total = grx[it, 0].astype(F32)
@@ -242,7 +259,7 @@
             current = fil32[...].reshape(kp, fil32.shape[2])
         if n_part > 1:
             wait_in(sqs.at[it, pl.ds(0, n_part - 1)], base + 3)
-        squares = jnp.sum(sqs[it], axis=0)[:1, :1]
+        squares = jnp.sum(sqs[it], axis=0)[:, :1]
         scale = jnp.sqrt(squares / count + EPSILON)
         moved = current - FILTER_STEP * gradient / scale
         lengths = jnp.sqrt(jnp.sum(moved * moved, axis=1, keepdims=True))
@@ -253,6 +270,7 @@
             fil32[...] = moved.reshape(fil32.shape)
             filters = moved.astype(BF16)
 
+    store.wait()
     if n_img > 1:
         wait_out(fil_bf.at[pl.ds(0, n_img - 1)], 0)
     for it in range(ITERS):
@@ -279,8 +297,9 @@
     share = -(-held // (16 * n_chan)) * 16 * n_chan
     kp = share * n_img
     lanes = -(-taps // LANES) * LANES
-    coef = coefficients.reshape(n_img, held, pixels)
-    coef = jnp.pad(coef, ((0, 0), (0, share - held), (0, 0))).reshape(kp, pixels)
+    coef = coefficients.reshape(n_img, held, height, width)
+    coef = jnp.pad(coef, ((0, 0), (0, share - held), (0, 0), (0, 0)))
+    coef = coef.reshape(kp, height, width)
     dictionary = jnp.pad(dictionary, ((0, share - held), (0, 0)))
     order = jnp.asarray(tap_order(taps, lanes))
     gr = GROUP * COLORS
@@ -288,21 +307,26 @@
     dtp_rows = gr + COLORS * (SIDE - 1) + gr + 2
     sems = 2 + 4 * ITERS
     vmem = pl.BlockSpec(memory_space=pltpu.VMEM)
+    hbm = pl.BlockSpec(memory_space=pl.ANY)
     out_coef, out_dict = pl.pallas_call(
         functools.partial(kernel, sizes, float(filters * n_filt * taps)),
         out_shape=(
-            jax.ShapeDtypeStruct((kp, pixels), BF16),
+            jax.ShapeDtypeStruct((kp, height, width), BF16),
             jax.ShapeDtypeStruct((share, taps), F32),
         ),
-        in_specs=[vmem, pl.BlockSpec(memory_space=pl.ANY), vmem, vmem],
-        out_specs=(vmem, vmem),
+        in_specs=[vmem, hbm, vmem, hbm],
+        out_specs=(hbm, vmem),
         scratch_shapes=[
+            pltpu.VMEM((kp, height, width), BF16),
             pltpu.VMEM((kp, (height + 2 * HALF) * width), BF16),
             pltpu.VMEM((ROWS, pixels), BF16),
             pltpu.VMEM((toep_rows, SPAN * kp), BF16),
             pltpu.VMEM((SIDE, dtp_rows, kp), F32),
             pltpu.VMEM((SIDE, COLORS * (height - 1) + BLOCK + 3, width), F32),
             pltpu.VMEM((COLORS * height, width), F32),
+            pltpu.VMEM((lanes, ROWS), BF16),
+            pltpu.VMEM((kp, 16, width), F32),
+            pltpu.VMEM((kp, height, width), BF16),
             pltpu.VMEM((n_img, share, lanes), BF16),
             pltpu.VMEM((n_img, share, lanes), F32),
             pltpu.VMEM((ITERS, n_filt, COLORS * height, width), F32),
@@ -310,8 +334,8 @@
             pltpu.VMEM((ITERS, n, share // n_chan, lanes), BF16),
             pltpu.VMEM((ITERS - 1, n, share // n_chan, lanes), BF16),
             pltpu.VMEM((n_chan, share // n_chan, lanes), BF16),
-            pltpu.VMEM((ITERS, n * n_filt, 8, LANES), F32),
-            pltpu.SemaphoreType.DMA,
+            pltpu.VMEM((ITERS, n * n_filt, 1, LANES), F32),
+            pltpu.SemaphoreType.DMA((2,)),
             pltpu.SemaphoreType.DMA((sems,)),
             pltpu.SemaphoreType.DMA((sems,)),
         ],

time: 49.7 us -> 44 us (0.89)
  Pallas kernels: 43.2 us -> 40.2 us
  local copies, waits for them, and re-layouts: 5.71 us -> 2.9 us
    pallas_call x1, Pallas kernels: 43.2 us -> 40.2 us  [per_device(): pl.pallas_call(functools.partial(kernel, sizes, float(filters * n_filt *...]
    unnamed x5 -> x4, local copies, waits for them, and re-layouts: 5.71 us -> 2.9 us
where the time goes in v1:
time: 44 us; the launch traced here: 43.8 us
  Pallas kernels  40.2 us (91%)
  local copies, waits for them, and re-layouts  2.9 us (7%)
  between operations  0.65 us (1%)
    pallas_call x1, Pallas kernels, per_device(): pl.pallas_call(functools.partial(kernel, sizes, float(filters * n_filt *...  40.2 us
    unnamed x4, local copies, waits for them, and re-layouts  2.9 us

profile of v1, /device:TPU:0, one launch (start us, length us, event | category | flops | bytes accessed | tf_op | source)
XLA Modules:
  0.0 43.8 jit_solution(3991332745086617640)
XLA Ops:
  0.6 40.2 %dictionary_steps.1 = (bf16[128,32,128]{2,1,0:T(8,128)(2,1)}, f32[32,363]{1,0:T(8,128)}) custom-call(f32[3,32,128]{2,1,0:T(8,128)} %bitcast.5, bf16[128,32,128]{2,1,0:T(8,128)(2,1)} %bitcast.3, f32[32,363]{1,0:T(8,128)} %dict_ref.1, bf16[384,448]{1,0:T(8,128)(2,1)} %constant.1.clone.order_hbm), custom_call_target="tpu_custom_call" | custom-call | tf_op jit(solution)/shard_map/dictionary_steps/pallas_call | solution.py:311
  40.9 0.0 copy-start
  40.9 2.3 %copy.8 = bf16[1,128,32,128]{3,2,1,0:T(8,128)(2,1)} copy(bf16[1,128,32,128]{3,2,1,0:T(8,128)(2,1)} %bitcast.4) | data formatting | bytes 2097152
  43.2 0.0 copy-done
  43.2 0.6 %copy.9 = f32[32,363]{1,0:T(8,128)} copy(f32[32,363]{1,0:T(8,128)S(1)} %copy-done) | data formatting | bytes 92928
Async XLA Ops:
  40.9 2.3 %copy-start = (f32[32,363]{1,0:T(8,128)S(1)}, f32[32,363]{1,0:T(8,128)}, u32[]{:S(2)}) copy-start(f32[32,363]{1,0:T(8,128)} %get-tuple-element.9) | copy-start | bytes 139396

commit v2 on v1

--- a/solution.py
+++ b/solution.py
@@ -175,7 +175,7 @@
             ], 0)
             term = roll_columns(block, col - HALF)
             share_sum = term if share_sum is None else share_sum + term
-        rec[it, filt] = share_sum
+        rec[it, filt] = share_sum.astype(BF16)
         for d in filt_peers():
             push(rec.at[it, filt], rec.at[it, filt], base, d)
         if it == 0:
@@ -183,9 +183,9 @@
                 push(fil32.at[img], fil32.at[img], 1, d)
         if n_filt > 1:
             wait_in(rec.at[it, pl.ds(0, n_filt - 1)], base)
-        recon = rec[it, 0]
-        for f in range(1, n_filt):
-            recon = recon + rec[it, f]
+        recon = share_sum
+        for s in range(1, n_filt):
+            recon = recon + rec[it, lax.rem(filt + s, n_filt)].astype(F32)
         resid = (recon - image_rows[...]).astype(BF16).astype(F32)
 
         for col in range(SIDE):
@@ -237,8 +237,8 @@
         total = total_bf.astype(F32)
         square = jnp.sum(jnp.sum(total * total, axis=1, keepdims=True), axis=0, keepdims=True)
         sqs[it, me_part] = jnp.broadcast_to(square, sqs.shape[2:])
-        part_loop(lambda d: push(sqs.at[it, me_part], sqs.at[it, me_part], base + 3, d))
         if last:
+            part_loop(lambda d: push(sqs.at[it, me_part], sqs.at[it, me_part], base + 3, d))
             glast[chan] = total_bf
             for d in chan_peers():
                 push(glast.at[chan], glast.at[chan], base + 2, d)
@@ -250,6 +250,7 @@
             gall[it, me] = total_bf
             for other, d in set_peers():
                 push(gall.at[it, me], gall.at[it, me], base + 2, d)
+            part_loop(lambda d: push(sqs.at[it, me_part], sqs.at[it, me_part], base + 3, d))
             if it == 0 and n_img > 1:
                 wait_in(fil32.at[pl.ds(0, n_img - 1)], 1)
                 wait_out(fil32.at[pl.ds(0, n_img - 1)], 1)
@@ -329,7 +330,7 @@
             pltpu.VMEM((kp, height, width), BF16),
             pltpu.VMEM((n_img, share, lanes), BF16),
             pltpu.VMEM((n_img, share, lanes), F32),
-            pltpu.VMEM((ITERS, n_filt, COLORS * height, width), F32),
+            pltpu.VMEM((ITERS, n_filt, COLORS * height, width), BF16),
             pltpu.VMEM((ITERS, n, share // n_chan, lanes), BF16),
             pltpu.VMEM((ITERS, n, share // n_chan, lanes), BF16),
             pltpu.VMEM((ITERS - 1, n, share // n_chan, lanes), BF16),

time: 44 us -> 44.9 us (1.020)
  Pallas kernels: 40.2 us -> 41.1 us
    pallas_call x1, Pallas kernels: 40.2 us -> 41.1 us  [per_device(): pl.pallas_call(functools.partial(kernel, sizes, float(filters * n_filt *...]
where the time goes in v2:
time: 44.9 us; the launch traced here: 44.7 us
  Pallas kernels  41.1 us (92%)
  local copies, waits for them, and re-layouts  2.9 us (6%)
  between operations  0.65 us (1%)
    pallas_call x1, Pallas kernels, per_device(): pl.pallas_call(functools.partial(kernel, sizes, float(filters * n_filt *...  41.1 us
    unnamed x4, local copies, waits for them, and re-layouts  2.9 us

profile of v2, /device:TPU:0, one launch (start us, length us, event | category | flops | bytes accessed | tf_op | source)
XLA Modules:
  0.0 44.7 jit_solution(3479313667877640437)
XLA Ops:
  0.6 41.1 %dictionary_steps.1 = (bf16[128,32,128]{2,1,0:T(8,128)(2,1)}, f32[32,363]{1,0:T(8,128)}) custom-call(f32[3,32,128]{2,1,0:T(8,128)} %bitcast.5, bf16[128,32,128]{2,1,0:T(8,128)(2,1)} %bitcast.3, f32[32,363]{1,0:T(8,128)} %dict_ref.1, bf16[384,448]{1,0:T(8,128)(2,1)} %constant.1.clone.order_hbm), custom_call_target="tpu_custom_call" | custom-call | tf_op jit(solution)/shard_map/dictionary_steps/pallas_call | solution.py:312
  41.8 0.0 copy-start
  41.8 2.3 %copy.8 = bf16[1,128,32,128]{3,2,1,0:T(8,128)(2,1)} copy(bf16[1,128,32,128]{3,2,1,0:T(8,128)(2,1)} %bitcast.4) | data formatting | bytes 2097152
  44.1 0.0 copy-done
  44.1 0.6 %copy.9 = f32[32,363]{1,0:T(8,128)} copy(f32[32,363]{1,0:T(8,128)S(1)} %copy-done) | data formatting | bytes 92928
Async XLA Ops:
  41.8 2.3 %copy-start = (f32[32,363]{1,0:T(8,128)S(1)}, f32[32,363]{1,0:T(8,128)}, u32[]{:S(2)}) copy-start(f32[32,363]{1,0:T(8,128)} %get-tuple-element.9) | copy-start | bytes 139396
